TPU v7x, 768 devices: a whole 4x8x12 slice. The times are simulated.
768 devices in a mesh: aux: 64 (over y, x, core), occ: 12 (over z).
Axes of the slice: x: 4, y: 8, z: 12, core: 2. Of those that a mesh axis runs over, the one named last changes fastest.
Arguments:
- aux_tiles: bfloat16 [256, 64, 128, 128], P('aux'), may hold values from -0.5 to 0.5
- orbitals: bfloat16 [48, 5376], P('occ'), may hold values from -0.29882812 to 0.29882812
- tile_rows: int32 [64, 64], P('aux'), may hold values from 0 to 41, as said below
- tile_cols: int32 [64, 64], P('aux'), may hold values from 0 to 41
- tile_count: int32 [64], P('aux'), may hold values from 42 to 64, as said below
Outputs:
- exchange: float32 [5376, 5376], P('aux', 'occ')
Inputs may be any that keep to these rules, and one draw needn't show every extreme that they name: `tile_rows`: in every slab the first 42 slots name each row block once. `tile_count`: some slab has all 64 slots live and some slab exactly 42.
All inputs are finite; a program needn't handle non-finite values.
Results may differ from a plain program's by a relative error of at most 0.0027.
Values may be sent and summed in bfloat16 or wider, within the bound.
A program may use at most 64 MiB of HBM per device.

v0:
```python
import jax
import jax.numpy as jnp
from jax import lax
from jax.sharding import PartitionSpec as P


def per_device(aux_tiles, orbitals, tile_rows, tile_cols, tile_count):
    occ_local = orbitals.shape[0]
    basis = orbitals.shape[1]
    tile_size = aux_tiles.shape[2]
    slots = aux_tiles.shape[1]
    blocks_all = basis // tile_size
    slab_rows = tile_rows[0]
    slab_cols = tile_cols[0]
    orb_blocks = orbitals.reshape(occ_local, blocks_all, tile_size)[:, slab_cols, :]
    half_tile = jnp.einsum(
        "ptmn,itn->itpm", aux_tiles, orb_blocks, preferred_element_type=jnp.float32
    )
    live_tiles = (jnp.arange(slots, dtype=jnp.int32) < tile_count[0]).astype(jnp.float32)
    onehot = (slab_rows[:, None] == jnp.arange(blocks_all, dtype=jnp.int32)[None, :]).astype(
        jnp.float32
    ) * live_tiles[:, None]
    placed = jnp.einsum("tb,itpm->ipbm", onehot, half_tile, precision=lax.Precision.HIGHEST)
    half_vals = placed.reshape(occ_local, aux_tiles.shape[0], basis).astype(jnp.bfloat16)
    relaid = lax.all_to_all(half_vals, "aux", split_axis=2, concat_axis=1, tiled=True)
    partial_rows = jnp.einsum(
        "ipm,ipn->mn",
        relaid,
        lax.all_gather(relaid, "aux", axis=2, tiled=True),
        preferred_element_type=jnp.float32,
    )
    return lax.psum_scatter(partial_rows, "occ", scatter_dimension=1, tiled=True)


def solution(mesh):
    return jax.shard_map(
        per_device,
        mesh=mesh,
        in_specs=(
            P("aux", None, None, None),
            P("occ", None),
            P("aux", None),
            P("aux", None),
            P("aux"),
        ),
        out_specs=P("aux", "occ"),
        check_vma=False,
    )
```

profile of v0, /device:TPU:6, one launch (start us, length us, event | category | flops | bytes accessed | tf_op | source)
XLA Modules:
  0.0 239.4 jit_solution(3343642870560443952)
XLA Ops:
  6.5 0.0 copy-start
  6.5 0.0 copy-start.1
  6.5 0.0 all-gather.2.cloned.1.call-start
  7.2 0.7 fusion.18
  7.9 0.0 copy-done
  7.9 0.7 gather_fusion
  8.5 5.6 %fusion.7 = f32[4,64,4,128]{3,0,2,1:T(4,128)S(1)} fusion(bf16[4,64,128,128]{3,2,1,0:T(8,128)(2,1)} %param.5, bf16[64,4,128]{2,1,0:T(4,128)(2,1)S(1)} %gather_fusion), kind=kOutput, calls=%fused_computation.6 | convolution fusion | flops 33554432 | bytes 8978432 | tf_op jit(solution)/shard_map/ptmn,itn->itpm/dot_general | solution.py:16
  14.2 0.0 copy-done.1
  14.2 0.7 fusion.10
  14.9 4.8 %copy.22 = bf16[4,4,42,128]{1,0,3,2:T(4,128)(2,1)} copy(bf16[4,4,42,128]{3,2,1,0:T(8,128)(2,1)S(1)} %fusion.10) | data formatting | bytes 344064 | tf_op jit(solution)/shard_map/convert_element_type | solution.py:24
  19.7 7.5 %reshape.53 = bf16[64,2,672]{2,1,0:T(2,128)(2,1)S(1)} reshape(bf16[5376,4,4]{2,1,0:T(4,128)(2,1)} %bitcast.39) | data formatting | bytes 344064
  27.2 23.4 %all_to_all.18 = bf16[64,2,672]{2,1,0:T(2,128)(2,1)S(1)} all-to-all(bf16[64,2,672]{2,1,0:T(2,128)(2,1)S(1)} %reshape.53), channel_id=1, replica_groups=mesh['aux'=64,'occ'=12] {'aux'}, dimensions={0} | all-to-all | bytes 344064 | tf_op jit(solution)/shard_map/all_to_all | solution.py:25
  50.6 5.0 %reshape.54 = bf16[5376,4,4]{2,1,0:T(4,128)(2,1)} reshape(bf16[64,2,672]{2,1,0:T(2,128)(2,1)S(1)} %all_to_all.18) | data formatting | bytes 344064
  55.5 6.7 %copy.15 = bf16[4,4,64,84]{3,1,2,0:T(4,128)(2,1)S(1)} copy(bf16[4,4,64,84]{1,0,3,2:T(4,128)(2,1)} %bitcast.40) | data formatting | bytes 344064 | tf_op jit(solution)/shard_map/all_to_all | solution.py:25
  62.2 0.9 copy.16
  63.1 0.0 all-gather.2.cloned.1.call-update
  63.1 0.0 reduce-scatter.4.cloned.1.call-start
  63.2 95.7 %all-gather.2.cloned.1.call-done = bf16[4,256,5376]{1,0,2:T(4,128)(2,1)} async-done(((bf16[4,256,84]{1,0,2:T(4,128)(2,1)}), bf16[4,256,5376]{1,0,2:T(4,128)(2,1)}) %all-gather.2.cloned.1.call-update) | async-done | bytes 11010064 | tf_op jit(solution)/shard_map/all_gather | solution.py:29
  158.9 8.8 %fusion.4 = f32[5376,84]{1,0:T(8,128)} fusion(bf16[4,256,84]{2,1,0:T(8,128)(2,1)S(1)} %bitcast.42, bf16[4,256,5376]{1,0,2:T(4,128)(2,1)} %all-gather.2.cloned.1.call-done), kind=kOutput, calls=%fused_computation.5 | convolution fusion | flops 924844032 | bytes 12988416 | tf_op jit(solution)/shard_map/ipm,ipn->mn/dot_general | solution.py:26
  167.6 0.0 reduce-scatter.4.cloned.1.call-update
  167.7 63.2 %reduce-scatter.4.cloned.1.call-done = f32[448,84]{1,0:T(8,128)} async-done(((f32[5376,84]{1,0:T(8,128)}), f32[448,84]{1,0:T(8,128)}) %reduce-scatter.4.cloned.1.call-update) | async-done | bytes 150544
  230.8 1.7 copy.24
  (2 shorter events, 0.0 us)
Async XLA Ops:
  6.5 1.4 copy-start
  6.5 7.6 %copy-start.1 = (s32[1,64]{1,0:T(1,128)S(1)}, s32[1,64]{1,0:T(1,128)}, u32[]{:S(2)}) copy-start(s32[1,64]{1,0:T(1,128)} %param.7) | copy-start | bytes 772
  6.5 152.3 %all-gather.2.cloned.1.call-start = ((), (), s32[]{:S(2)}) async-start(), calls=%async_computation.2 | async-start | bytes 11182080 | tf_op jit(solution)/shard_map/all_gather | solution.py:29
  63.1 167.7 %reduce-scatter.4.cloned.1.call-start = ((), (), s32[]{:S(2)}) async-start(), calls=%async_computation.3 | async-start | bytes 2981888
Sparse Core Ops, SparseCore 0:
  63.2 95.5 all-gather.1
  167.8 63.0 reduce-scatter.3
where the time goes:
time: 240 us; the launch traced here: 239 us
  waiting for transfers between devices  159 us (66%)
  local copies, waits for them, and re-layouts  27.2 us (11%)
  blocking collectives  23.4 us (10%)
  matrix products  15.1 us (6%)
  between operations  14.1 us (6%)
    all_gather x1, waiting for transfers between devices, per_device(): lax.all_gather(relaid, 'aux', axis=2, tiled=True)  95.7 us
    unnamed x3, waiting for transfers between devices  63.2 us
    all_to_all x1, blocking collectives, per_device(): lax.all_to_all(half_vals, 'aux', split_axis=2, concat_axis=1, tiled=True)  23.4 us
    unnamed x7, local copies, waits for them, and re-layouts  14.2 us
    dot_general x1, matrix products, per_device(): jnp.einsum('ipm,ipn->mn', relaid, lax.all_gather(relaid, 'aux', axis=2, t...  8.78 us
    all_to_all x2, local copies, waits for them, and re-layouts, per_device(): lax.all_to_all(half_vals, 'aux', split_axis=2, concat_axis=1, tiled=True)  7.53 us
    dot_general x1, matrix products, per_device(): jnp.einsum('ptmn,itn->itpm', aux_tiles, orb_blocks, preferred_element_typ...  5.64 us
  transfers between devices with their start and end apart: 2, of which 2 were waited for; matrix products, arithmetic and copies ran while one was open for 0% of the time, Pallas kernels for 0%

commit v1 on v0

v1 whole, which is shorter than its diff:
```python
import functools

import jax
import jax.numpy as jnp
from jax import lax
from jax.experimental import pallas as pl
from jax.experimental.pallas import tpu as pltpu
from jax.sharding import PartitionSpec as P

MESH = pl.DeviceIdType.MESH
TILE = 128
NB = 42
NT = 64
PD = 4
OL = 4
BASIS = NB * TILE
NX, NY, NC, NZ = 4, 8, 2, 12
ROWS = 84
COLS = 448
SEG = COLS // NX
GROUP = (64, 48)
LANES = (768, 640)
BASE = (0, 768)
XW = 1408
YH = 384
YW = 2 * YH
KP = PD * OL
SLOTS_STEP = 8


def half_kernel(rows_ref, cols_ref, count_ref, tiles_ref, orb_ref, hx_ref, hy_ref, acc, flat):
    step = pl.program_id(0)

    @pl.when(step == 0)
    def _():
        acc[...] = jnp.zeros_like(acc)

    for s in range(SLOTS_STEP):
        t = step * SLOTS_STEP + s
        row = rows_ref[0, t]
        col = cols_ref[0, t]
        block = orb_ref[:, pl.ds(pl.multiple_of(col * TILE, TILE), TILE)]
        tile = tiles_ref[:, s].reshape(PD * TILE, TILE)
        got = lax.dot_general(block, tile, (((1,), (1,)), ((), ())), preferred_element_type=jnp.float32)
        live = (t < count_ref[0]).astype(jnp.float32)
        acc[row] += got * live

    @pl.when(step == pl.num_programs(0) - 1)
    def _():
        for b in range(NB):
            for p in range(PD):
                flat[p * OL:(p + 1) * OL, b * TILE:(b + 1) * TILE] = acc[b, :, p * TILE:(p + 1) * TILE]
        for x in range(NX):
            parts = []
            for g, start in ((0, 0), (1, GROUP[0])):
                for o in range(NZ):
                    a = o * COLS + x * SEG + start
                    parts.append(flat[:, a:a + GROUP[g]])
            parts.append(jnp.zeros((KP, XW - NZ * SEG), jnp.float32))
            hx_ref[x] = jnp.concatenate(parts, axis=1).astype(jnp.bfloat16)
        for y in range(NY):
            parts = []
            for c in range(NC):
                for x in range(NX):
                    a = ((y * NX + x) * NC + c) * ROWS
                    parts.append(flat[:, a:a + ROWS])
                parts.append(jnp.zeros((KP, YH - NX * ROWS), jnp.float32))
            hy_ref[y] = jnp.concatenate(parts, axis=1).astype(jnp.bfloat16)


def half(aux_tiles, orbitals, tile_rows, tile_cols, tile_count):
    smem = pl.BlockSpec(memory_space=pltpu.SMEM)
    return pl.pallas_call(
        half_kernel,
        grid=(NT // SLOTS_STEP,),
        in_specs=[
            smem, smem, smem,
            pl.BlockSpec((PD, SLOTS_STEP, TILE, TILE), lambda i: (0, i, 0, 0)),
            pl.BlockSpec((OL, BASIS), lambda i: (0, 0)),
        ],
        out_specs=[
            pl.BlockSpec((NX, KP, XW), lambda i: (0, 0, 0)),
            pl.BlockSpec((NY, KP, YW), lambda i: (0, 0, 0)),
        ],
        out_shape=[
            jax.ShapeDtypeStruct((NX, KP, XW), jnp.bfloat16),
            jax.ShapeDtypeStruct((NY, KP, YW), jnp.bfloat16),
        ],
        scratch_shapes=[
            pltpu.VMEM((NB, OL, PD * TILE), jnp.float32),
            pltpu.VMEM((KP, BASIS), jnp.float32),
        ],
        compiler_params=pltpu.CompilerParams(vmem_limit_bytes=32 * 2**20),
    )(tile_rows, tile_cols, tile_count, aux_tiles, orbitals)


def exchange_kernel(
    hx_ref, hy_ref, out_ref,
    hx, hy, part, own, sib_out, sib_in, minus_out, minus_in, plus_out, plus_in, final_out, final_in,
    local_sem, x_send, x_recv, y_send, y_recv, ring_send, ring_recv, row_send, row_recv,
    sib_send, sib_recv, minus_send, minus_recv, plus_send, plus_recv, fin_send, fin_recv,
):
    aux = lax.axis_index("aux")
    z = lax.axis_index("occ")
    c = lax.rem(aux, NC)
    x = lax.rem(aux // NC, NX)
    y = aux // (NC * NX)

    def at(y_, x_, c_, z_):
        return ((y_ * NX + x_) * NC + c_, z_)

    def xp(d):
        return lax.rem(x + d, NX)

    def yp(d):
        return lax.rem(y + d, NY)

    def zp(d):
        return lax.rem(z + d, NZ)

    partners = [at(y, xp(d), c, z) for d in range(1, NX)]
    partners += [at(yp(d), x, c, z) for d in range(1, NY)]
    partners += [at(y, x, 1 - c, z), at(y, x, c, zp(1)), at(y, x, c, zp(NZ - 1))]
    barrier = pltpu.get_barrier_semaphore()
    for partner in partners:
        pl.semaphore_signal(barrier, inc=1, device_id=partner, device_id_type=MESH)
    pl.semaphore_wait(barrier, len(partners))

    waits = []

    def send(src, dst, s_sem, r_sem, device):
        copy = pltpu.make_async_remote_copy(
            src_ref=src, dst_ref=dst, send_sem=s_sem, recv_sem=r_sem, device_id=device, device_id_type=MESH)
        copy.start()
        waits.append(copy)
        return copy

    own_x = pltpu.make_async_copy(hx_ref.at[x], hx.at[y, x], local_sem.at[0])
    own_y = pltpu.make_async_copy(hy_ref.at[y], hy.at[y, x], local_sem.at[1])
    own_x.start()
    own_y.start()
    to_x = [send(hx_ref.at[xp(d)], hx.at[y, x], x_send.at[d - 1], x_recv.at[d - 1], at(y, xp(d), c, z))
            for d in range(1, NX)]
    to_y = [send(hy_ref.at[yp(d)], hy.at[y, x], y_send.at[d - 1], y_recv.at[d - 1], at(yp(d), x, c, z))
            for d in (1, 7, 2, 6, 3, 5, 4)]
    own_x.wait()
    for copy in to_x:
        copy.wait_recv()

    up, down = at(yp(1), x, c, z), at(yp(NY - 1), x, c, z)

    def ring(g, step):
        lanes = pl.ds(BASE[g], LANES[g])
        a, b = yp(NY - step), yp(step)
        if step < NY // 2 - 1:
            up_ref, down_ref = hx.at[a, :, :, lanes], hx.at[b, :, :, lanes]
        else:
            up_ref, down_ref = hx.at[a, 0:2, :, lanes], hx.at[b, 2:4, :, lanes]
        return (send(up_ref, up_ref, ring_send.at[0, g, step], ring_recv.at[0, g, step], up),
                send(down_ref, down_ref, ring_send.at[1, g, step], ring_recv.at[1, g, step], down))

    rings = {}
    rings[0, 0] = ring(0, 0)

    own_y.wait()
    for copy in to_y:
        copy.wait_recv()
    right, left = at(y, xp(1), c, z), at(y, xp(NX - 1), c, z)
    row0 = (send(hy.at[:, x], hy.at[:, x], row_send.at[0], row_recv.at[0], right),
            send(hy.at[:, x], hy.at[:, x], row_send.at[1], row_recv.at[1], left))

    for step in range(1, 4):
        for copy in rings[0, step - 1]:
            copy.wait_recv()
        rings[0, step] = ring(0, step)
        if step == 1:
            for copy in row0:
                copy.wait_recv()
            a, b = hy.at[0:4, xp(3)], hy.at[4:8, xp(1)]
            row1 = (send(a, a, row_send.at[2], row_recv.at[2], right),
                    send(b, b, row_send.at[3], row_recv.at[3], left))
    rings[1, 0] = ring(1, 0)
    for copy in row1:
        copy.wait_recv()
    for copy in rings[0, 3]:
        copy.wait_recv()

    minus, plus = at(y, x, c, zp(NZ - 1)), at(y, x, c, zp(1))
    sibling = at(y, x, 1 - c, z)
    result = []
    for g in range(2):
        size, lanes = GROUP[g], LANES[g]
        if g == 1:
            for copy in rings[1, 3]:
                copy.wait_recv()
        hy_all = hy[...].reshape(NY * NX * KP, YW)
        for j in range(0, lanes, TILE):
            hx_all = hx[:, :, :, BASE[g] + j:BASE[g] + j + TILE].reshape(NY * NX * KP, TILE)
            part[j:j + TILE, :] = lax.dot_general(
                hx_all, hy_all, (((0,), (0,)), ((), ())), preferred_element_type=jnp.float32)
        if g == 0:
            for copy in rings[1, 0]:
                copy.wait_recv()
            rings[1, 1] = ring(1, 1)
        mine = pl.ds(pl.multiple_of(c * YH, TILE), YH)
        other = pl.ds(pl.multiple_of((1 - c) * YH, TILE), YH)
        used = NZ * size
        sib_out[0:used, :] = part[0:used, other].astype(jnp.bfloat16)
        copy = send(sib_out.at[0:used], sib_in.at[g, 0:used], sib_send.at[g], sib_recv.at[g], sibling)
        copy.wait_recv()
        own[g, 0:used, :] = part[0:used, mine] + sib_in[g, 0:used, :].astype(jnp.float32)
        if g == 0:
            copy.wait_send()
            waits[:] = [w for w in waits if w is not copy]

        def piece(o, g=g, size=size):
            return own[g, pl.ds(pl.multiple_of(o * size, 16), size), :]

        before = None
        for step in range(6):
            now = []
            if before is not None:
                before[0].wait_recv()
            value = piece(zp(NZ - 6 + step))
            if before is not None:
                value = value + minus_in[g, step - 1, 0:size, :].astype(jnp.float32)
            minus_out[g, step, 0:size, :] = value.astype(jnp.bfloat16)
            now.append(send(minus_out.at[g, step, 0:size], minus_in.at[g, step, 0:size],
                            minus_send.at[g, step], minus_recv.at[g, step], minus))
            if step < 5:
                if before is not None:
                    before[1].wait_recv()
                value = piece(zp(5 - step))
                if before is not None:
                    value = value + plus_in[g, step - 1, 0:size, :].astype(jnp.float32)
                plus_out[g, step, 0:size, :] = value.astype(jnp.bfloat16)
                now.append(send(plus_out.at[g, step, 0:size], plus_in.at[g, step, 0:size],
                                plus_send.at[g, step], plus_recv.at[g, step], plus))
            elif before is not None:
                before[1].wait_recv()
            before = now
            if g == 0 and step in (1, 3):
                for copy in rings[1, 1 + step // 2]:
                    copy.wait_recv()
                rings[1, 2 + step // 2] = ring(1, 2 + step // 2)
        before[0].wait_recv()
        result.append(piece(z) + minus_in[g, 5, 0:size, :].astype(jnp.float32)
                      + plus_in[g, 4, 0:size, :].astype(jnp.float32))

    whole = jnp.concatenate(result, axis=0)
    for q in range(NX):
        final_out[q, :, 0:ROWS] = whole[:, q * ROWS:(q + 1) * ROWS]
        final_out[q, :, ROWS:TILE] = jnp.zeros((SEG, TILE - ROWS), jnp.float32)
    last = [send(final_out.at[xp(d)], final_in.at[x], fin_send.at[d - 1], fin_recv.at[d - 1], at(y, xp(d), c, z))
            for d in range(1, NX)]
    final_in[x] = final_out[x]
    for copy in last:
        copy.wait_recv()
    out_ref[...] = final_in[...].reshape(COLS, TILE).T[0:ROWS]
    for copy in waits:
        copy.wait_send()


def exchange(hx, hy):
    vmem = pl.BlockSpec(memory_space=pltpu.VMEM)
    dma = pltpu.SemaphoreType.DMA
    f32, bf16 = jnp.float32, jnp.bfloat16
    return pl.pallas_call(
        exchange_kernel,
        out_shape=jax.ShapeDtypeStruct((ROWS, COLS), f32),
        in_specs=[vmem, vmem],
        out_specs=vmem,
        scratch_shapes=[
            pltpu.VMEM((NY, NX, KP, XW), bf16),
            pltpu.VMEM((NY, NX, KP, YW), bf16),
            pltpu.VMEM((LANES[0], YW), f32),
            pltpu.VMEM((2, LANES[0], YH), f32),
            pltpu.VMEM((LANES[0], YH), bf16),
            pltpu.VMEM((2, LANES[0], YH), bf16),
            pltpu.VMEM((2, 6, GROUP[0], YH), bf16),
            pltpu.VMEM((2, 6, GROUP[0], YH), bf16),
            pltpu.VMEM((2, 5, GROUP[0], YH), bf16),
            pltpu.VMEM((2, 5, GROUP[0], YH), bf16),
            pltpu.VMEM((NX, SEG, TILE), f32),
            pltpu.VMEM((NX, SEG, TILE), f32),
            dma((2,)), dma((3,)), dma((3,)), dma((7,)), dma((7,)),
            dma((2, 2, 4)), dma((2, 2, 4)), dma((4,)), dma((4,)),
            dma((2,)), dma((2,)), dma((2, 6)), dma((2, 6)), dma((2, 5)), dma((2, 5)),
            dma((3,)), dma((3,)),
        ],
        compiler_params=pltpu.CompilerParams(
            collective_id=0, has_side_effects=True, vmem_limit_bytes=48 * 2**20),
    )(hx, hy)


def per_device(aux_tiles, orbitals, tile_rows, tile_cols, tile_count):
    hx, hy = half(aux_tiles, orbitals, tile_rows, tile_cols, tile_count)
    return exchange(hx, hy)


def solution(mesh):
    return jax.shard_map(
        per_device,
        mesh=mesh,
        in_specs=(
            P("aux", None, None, None),
            P("occ", None),
            P("aux", None),
            P("aux", None),
            P("aux"),
        ),
        out_specs=P("aux", "occ"),
        check_vma=False,
    )
```

time: 240 us -> 99.6 us (0.41)
  waiting for transfers between devices: 159 us -> 0 us
  Pallas kernels: 0 us -> 91.9 us
  blocking collectives: 23.4 us -> 0 us
  local copies, waits for them, and re-layouts: 27.2 us -> 6.14 us
  matrix products: 15.1 us -> 0 us
  between operations: 14.1 us -> 0.68 us
    all_gather x1 -> x0, waiting for transfers between devices: 95.7 us -> none  [per_device(): lax.all_gather(relaid, 'aux', axis=2, tiled=True)]
    pallas_call x0 -> x2, Pallas kernels: none -> 91.9 us  [the longest x1 87.4 us: exchange(): pl.pallas_call(exchange_kernel, out_shape=jax.ShapeDtypeStruct((ROWS, COL...]
    unnamed x3 -> x0, waiting for transfers between devices: 63.2 us -> none
    all_to_all x1 -> x0, blocking collectives: 23.4 us -> none  [per_device(): lax.all_to_all(half_vals, 'aux', split_axis=2, concat_axis=1, tiled=True)]
    dot_general x3 -> x0, matrix products: 15.1 us -> none  [the longest x1 8.78 us: per_device(): jnp.einsum('ipm,ipn->mn', relaid, lax.all_gather(relaid, 'aux', axis=2, t...]
    unnamed x7 -> x9, local copies, waits for them, and re-layouts: 14.2 us -> 6.14 us
    all_to_all x2 -> x0, local copies, waits for them, and re-layouts: 7.53 us -> none  [per_device(): lax.all_to_all(half_vals, 'aux', split_axis=2, concat_axis=1, tiled=True)]
    convert_element_type x1 -> x0, local copies, waits for them, and re-layouts: 4.78 us -> none  [per_device(): placed.reshape(occ_local, aux_tiles.shape[0], basis).astype(jnp.bfloat16)]
  transfers between devices with their start and end apart: 2 -> 0, of which waited for: 2 -> 0; matrix products, arithmetic and copies ran while one was open for 0% -> 0% of each run, Pallas kernels for 0% -> 0%
where the time goes in v1:
time: 99.6 us; the launch traced here: 98.7 us
  Pallas kernels  91.9 us (92%)
  local copies, waits for them, and re-layouts  6.14 us (6%)
    pallas_call x1, Pallas kernels, exchange(): pl.pallas_call(exchange_kernel, out_shape=jax.ShapeDtypeStruct((ROWS, COL...  87.4 us
    unnamed x9, local copies, waits for them, and re-layouts  6.14 us
    pallas_call x1, Pallas kernels, half(): pl.pallas_call(half_kernel, grid=(NT // SLOTS_STEP,), in_specs=[smem, sme...  4.57 us

profile of v1, /device:TPU:6, one launch (start us, length us, event | category | flops | bytes accessed | tf_op | source)
XLA Modules:
  0.0 98.7 jit_solution(7453188224847232820)
XLA Ops:
  0.7 0.0 copy-start
  0.7 3.4 %copy-done = bf16[4,64,128,128]{3,2,1,0:T(8,128)(2,1)S(1)} copy-done((bf16[4,64,128,128]{3,2,1,0:T(8,128)(2,1)S(1)}, bf16[4,64,128,128]{3,2,1,0:T(8,128)(2,1)}, u32[]{:S(2)}) %copy-start) | copy-done | bytes 8388632
  4.0 0.0 copy-start.1
  4.0 0.8 copy-done.1
  4.8 0.0 copy-start.2
  4.8 0.7 copy-done.2
  5.5 0.0 copy-start.3
  5.5 0.7 copy-done.3
  6.1 4.6 %shard_map.55 = (bf16[4,16,1408]{2,1,0:T(8,128)(2,1)S(1)}, bf16[8,16,768]{2,1,0:T(8,128)(2,1)S(1)}) custom-call(s32[1,64]{1,0:T(1,128)S(1)} %copy-done.2, s32[1,64]{1,0:T(1,128)S(1)} %copy-done.3, s32[1]{0:T(128)S(6)} %copy.7.count_ref, bf16[4,64,128,128]{3,2,1,0:T(8,128)(2,1)S(1)} %copy-done, bf16[4,5376]{1,0:T(4,128)(2,1)S(1)} %copy-done.1), custom_call_target="tpu_custom_call" | custom-call | tf_op jit(solution)/shard_map/pallas_call | solution.py:73
  10.7 87.4 %shard_map.56 = f32[84,448]{1,0:T(8,128)S(1)} custom-call(bf16[4,16,1408]{2,1,0:T(8,128)(2,1)S(1)} %get-tuple-element.7.hx_ref, bf16[8,16,768]{2,1,0:T(8,128)(2,1)S(1)} %get-tuple-element.8.hy_ref), custom_call_target="tpu_custom_call" | custom-call | tf_op jit(solution)/shard_map/pallas_call | solution.py:268
  98.1 0.7 copy.8
Async XLA Ops:
  0.7 3.4 %copy-start = (bf16[4,64,128,128]{3,2,1,0:T(8,128)(2,1)S(1)}, bf16[4,64,128,128]{3,2,1,0:T(8,128)(2,1)}, u32[]{:S(2)}) copy-start(bf16[4,64,128,128]{3,2,1,0:T(8,128)(2,1)} %tiles_ref.1) | copy-start | bytes 25165828
  4.0 0.8 copy-start.1
  4.8 0.7 copy-start.2
  5.5 0.7 copy-start.3

commit v2 on v0

v2 whole, which is shorter than its diff:
```python
import functools

import jax
import jax.numpy as jnp
from jax import lax
from jax.experimental import pallas as pl
from jax.experimental.pallas import tpu as pltpu
from jax.sharding import PartitionSpec as P

MESH = pl.DeviceIdType.MESH
TILE = 128
NB = 42
NT = 64
PD = 4
OL = 4
BASIS = NB * TILE
NX, NY, NC, NZ = 4, 8, 2, 12
ROWS = 84
COLS = 448
SEG = COLS // NX
GROUP = (64, 48)
LANES = (768, 640)
BASE = (0, 768)
XW = 1408
YH = 384
YW = 2 * YH
KP = PD * OL
SLOTS_STEP = 8
GATHER = (
    (((0, 1, False), (0, 2, False)), ((2, 1, False), (2, 2, True))),
    (((0, 1, False),), ((1, 1, False),), ((2, 1, False), (2, 2, True))),
)
THREE = ((5, 4), (3, 2), (4, 2), (2, 0), (1, 0))
TWO = ((4, 3), (5, 3), (3, 0), (2, 0), (1, 0))
EDGES = ((THREE + ((6, 4),), THREE), (TWO + ((6, 3),), TWO))


def level(edges, node):
    return max((1 + level(edges, source) for source, target in edges if target == node), default=0)


def half_kernel(
    rows_hbm, cols_hbm, count_hbm, tiles_hbm, orb_hbm, hx_ref, hy_ref,
    rows_ref, cols_ref, count_ref, tiles, orb, acc, flat, sem, tile_sem,
):
    small = [
        pltpu.make_async_copy(rows_hbm, rows_ref, sem.at[0]),
        pltpu.make_async_copy(cols_hbm, cols_ref, sem.at[1]),
        pltpu.make_async_copy(count_hbm, count_ref, sem.at[2]),
        pltpu.make_async_copy(orb_hbm, orb, sem.at[3]),
    ]
    for copy in small:
        copy.start()
    big = []
    for k in range(NT // SLOTS_STEP):
        cut = pl.ds(k * SLOTS_STEP, SLOTS_STEP)
        big.append(pltpu.make_async_copy(tiles_hbm.at[:, cut], tiles.at[:, cut], tile_sem.at[k]))
        big[-1].start()
    acc[...] = jnp.zeros_like(acc)
    for copy in small:
        copy.wait()
    for k in range(NT // SLOTS_STEP):
        big[k].wait()
        for s in range(SLOTS_STEP):
            t = k * SLOTS_STEP + s
            row = rows_ref[0, t]
            col = cols_ref[0, t]
            block = orb[:, pl.ds(pl.multiple_of(col * TILE, TILE), TILE)]
            tile = tiles[:, t].reshape(PD * TILE, TILE)
            got = lax.dot_general(block, tile, (((1,), (1,)), ((), ())), preferred_element_type=jnp.float32)
            if t < NB:
                acc[row] += got
            else:
                acc[row] += jnp.where(t < count_ref[0], got, 0.0)
    for b in range(NB):
        for p in range(PD):
            flat[p * OL:(p + 1) * OL, b * TILE:(b + 1) * TILE] = acc[b, :, p * TILE:(p + 1) * TILE]
    for x in range(NX):
        parts = []
        for g in range(len(GROUP)):
            for o in range(NZ):
                a = o * COLS + x * SEG + sum(GROUP[:g])
                parts.append(flat[:, a:a + GROUP[g]])
            if LANES[g] > NZ * GROUP[g]:
                parts.append(jnp.zeros((KP, LANES[g] - NZ * GROUP[g]), jnp.float32))
        hx_ref[x] = jnp.concatenate(parts, axis=1).astype(jnp.bfloat16)
    for y in range(NY):
        parts = []
        for c in range(NC):
            for x in range(NX):
                a = ((y * NX + x) * NC + c) * ROWS
                parts.append(flat[:, a:a + ROWS])
            parts.append(jnp.zeros((KP, YH - NX * ROWS), jnp.float32))
        hy_ref[y] = jnp.concatenate(parts, axis=1).astype(jnp.bfloat16)


def half(aux_tiles, orbitals, tile_rows, tile_cols, tile_count):
    anywhere = pl.BlockSpec(memory_space=pl.ANY)
    vmem = pl.BlockSpec(memory_space=pltpu.VMEM)
    dma = pltpu.SemaphoreType.DMA
    return pl.pallas_call(
        half_kernel,
        in_specs=[anywhere] * 5,
        out_specs=[vmem] * 2,
        out_shape=[
            jax.ShapeDtypeStruct((NX, KP, XW), jnp.bfloat16),
            jax.ShapeDtypeStruct((NY, KP, YW), jnp.bfloat16),
        ],
        scratch_shapes=[
            pltpu.SMEM((1, NT), jnp.int32),
            pltpu.SMEM((1, NT), jnp.int32),
            pltpu.SMEM((1,), jnp.int32),
            pltpu.VMEM((PD, NT, TILE, TILE), jnp.bfloat16),
            pltpu.VMEM((OL, BASIS), jnp.bfloat16),
            pltpu.VMEM((NB, OL, PD * TILE), jnp.float32),
            pltpu.VMEM((KP, BASIS), jnp.float32),
            dma((4,)), dma((NT // SLOTS_STEP,)),
        ],
        compiler_params=pltpu.CompilerParams(vmem_limit_bytes=60 * 2**20),
    )(tile_rows, tile_cols, tile_count, aux_tiles, orbitals)


def exchange_kernel(
    hx_ref, hy_ref, out_ref,
    hx, hy, own, sib_out, sib_in, tree_out, tree_in, final_out, final_in,
    local_sem, x_send, x_recv, y_send, y_recv, ring_send, ring_recv, row_send, row_recv,
    sib_send, sib_recv, tree_send, tree_recv, fin_send, fin_recv,
):
    aux = lax.axis_index("aux")
    z = lax.axis_index("occ")
    c = lax.rem(aux, NC)
    x = lax.rem(aux // NC, NX)
    y = aux // (NC * NX)
    sign = 1 - 2 * c

    def at(y_, x_, c_, z_):
        return ((y_ * NX + x_) * NC + c_, z_)

    def xp(d):
        return lax.rem(x + d + NX, NX)

    def yp(d):
        return lax.rem(y + d + NY, NY)

    def zp(d):
        return lax.rem(z + sign * d + NZ, NZ)

    partners = [at(y, xp(d), c, z) for d in range(1, NX)]
    partners += [at(yp(d), x, c, z) for d in range(1, NY)]
    partners += [at(y, x, c, zp(d)) for d in (1, 2, 3, -1, -2, -3)]
    partners += [at(y, x, 1 - c, z)]
    barrier = pltpu.get_barrier_semaphore()
    for partner in partners:
        pl.semaphore_signal(barrier, inc=1, device_id=partner, device_id_type=MESH)
    pl.semaphore_wait(barrier, len(partners))

    started = []

    def send(src, dst, s_sem, r_sem, device):
        copy = pltpu.make_async_remote_copy(
            src_ref=src, dst_ref=dst, send_sem=s_sem, recv_sem=r_sem, device_id=device, device_id_type=MESH)
        copy.start()
        started.append(copy)
        return copy

    def arrive(copies):
        for copy in copies:
            copy.wait_recv()

    own_x = pltpu.make_async_copy(hx_ref.at[x], hx.at[y, x], local_sem.at[0])
    own_y = pltpu.make_async_copy(hy_ref.at[y], hy.at[y, x], local_sem.at[1])
    own_x.start()
    own_y.start()
    to_x = [send(hx_ref.at[xp(d)], hx.at[y, x], x_send.at[d - 1], x_recv.at[d - 1], at(y, xp(d), c, z))
            for d in range(1, NX)]
    to_y = [send(hy_ref.at[yp(d)], hy.at[y, x], y_send.at[d - 1], y_recv.at[d - 1], at(yp(d), x, c, z))
            for d in (1, 7, 2, 6, 3, 5, 4)]
    own_x.wait()
    arrive(to_x)

    rings = {}

    def ring(g, stage):
        lanes = pl.ds(BASE[g], LANES[g])
        count = sum(len(s) for s in GATHER[g][:stage])
        copies = []
        for n, (behind, hops, halved) in enumerate(GATHER[g][stage]):
            for way, turn in ((0, 1), (1, -1)):
                chunk = yp(-turn * behind)
                if halved:
                    ref = hx.at[chunk, 2 * way:2 * way + 2, :, lanes]
                else:
                    ref = hx.at[chunk, :, :, lanes]
                copies.append(send(ref, ref, ring_send.at[way, g, count + n], ring_recv.at[way, g, count + n],
                                   at(yp(turn * hops), x, c, z)))
        rings[g, stage] = copies

    ring(0, 0)
    ring(1, 0)

    own_y.wait()
    arrive(to_y)
    right, left = at(y, xp(1), c, z), at(y, xp(-1), c, z)
    row0 = (send(hy.at[:, x], hy.at[:, x], row_send.at[0], row_recv.at[0], right),
            send(hy.at[:, x], hy.at[:, x], row_send.at[1], row_recv.at[1], left))
    arrive(rings[0, 0])
    ring(0, 1)
    arrive(row0)
    a, b = hy.at[0:4, xp(-1)], hy.at[4:8, xp(1)]
    row1 = (send(a, a, row_send.at[2], row_recv.at[2], right),
            send(b, b, row_send.at[3], row_recv.at[3], left))
    arrive(rings[1, 0])
    ring(1, 1)
    arrive(row1)

    sibling = at(y, x, 1 - c, z)
    sib = {}

    def product(g, core, j):
        hx_all = hx[:, :, :, BASE[g] + j:BASE[g] + j + TILE].reshape(NY * NX * KP, TILE)
        hy_all = hy[:, :, :, pl.ds(pl.multiple_of(core * YH, TILE), YH)].reshape(NY * NX * KP, YH)
        return lax.dot_general(hx_all, hy_all, (((0,), (0,)), ((), ())), preferred_element_type=jnp.float32)

    def multiply(g):
        used = NZ * GROUP[g]
        for j in range(0, LANES[g], TILE):
            sib_out[g, j:j + TILE, :] = product(g, 1 - c, j).astype(jnp.bfloat16)
        sib[g] = send(sib_out.at[g, 0:used], sib_in.at[g, 0:used], sib_send.at[g], sib_recv.at[g], sibling)
        for j in range(0, LANES[g], TILE):
            own[g, j:j + TILE, :] = product(g, c, j)

    def add_sibling(g):
        used = NZ * GROUP[g]
        arrive([sib[g]])
        own[g, 0:used, :] += sib_in[g, 0:used, :].astype(jnp.float32)

    trees = {}

    def piece(g, o):
        return own[g, pl.ds(pl.multiple_of(o * GROUP[g], 16), GROUP[g]), :]

    def gathered(g, way, node, value):
        for n, (source, target) in enumerate(EDGES[g][way]):
            if target == node:
                arrive([trees[g, way, n]])
                value = value + tree_in[g, way, n, 0:GROUP[g], :].astype(jnp.float32)
        return value

    def tree(g, depth):
        for way, turn in ((0, 1), (1, -1)):
            edges = EDGES[g][way]
            for n, (source, target) in enumerate(edges):
                if level(edges, source) == depth:
                    value = gathered(g, way, source, piece(g, zp(-turn * source)))
                    tree_out[g, way, n, 0:GROUP[g], :] = value.astype(jnp.bfloat16)
                    trees[g, way, n] = send(
                        tree_out.at[g, way, n, 0:GROUP[g]], tree_in.at[g, way, n, 0:GROUP[g]],
                        tree_send.at[g, way, n], tree_recv.at[g, way, n], at(y, x, c, zp(-turn * (source - target))))

    arrive(rings[0, 1])
    multiply(0)
    arrive(rings[1, 1])
    ring(1, 2)
    add_sibling(0)
    tree(0, 0)
    arrive(rings[1, 2])
    multiply(1)
    tree(0, 1)
    add_sibling(1)
    tree(1, 0)
    tree(0, 2)
    tree(1, 1)
    result = []
    for g in range(2):
        value = piece(g, z)
        for way in range(2):
            value = gathered(g, way, 0, value)
        result.append(value)

    whole = jnp.concatenate(result, axis=0)
    for q in range(NX):
        final_out[q, :, 0:ROWS] = whole[:, q * ROWS:(q + 1) * ROWS]
        final_out[q, :, ROWS:TILE] = jnp.zeros((SEG, TILE - ROWS), jnp.float32)
    last = [send(final_out.at[xp(d)], final_in.at[x], fin_send.at[d - 1], fin_recv.at[d - 1], at(y, xp(d), c, z))
            for d in range(1, NX)]
    final_in[x] = final_out[x]
    arrive(last)
    out_ref[...] = final_in[...].reshape(COLS, TILE).T[0:ROWS]
    for copy in started:
        copy.wait_send()


def exchange(hx, hy):
    vmem = pl.BlockSpec(memory_space=pltpu.VMEM)
    dma = pltpu.SemaphoreType.DMA
    f32, bf16 = jnp.float32, jnp.bfloat16
    return pl.pallas_call(
        exchange_kernel,
        out_shape=jax.ShapeDtypeStruct((ROWS, COLS), f32),
        in_specs=[vmem, vmem],
        out_specs=vmem,
        scratch_shapes=[
            pltpu.VMEM((NY, NX, KP, XW), bf16),
            pltpu.VMEM((NY, NX, KP, YW), bf16),
            pltpu.VMEM((2, LANES[0], YH), f32),
            pltpu.VMEM((2, LANES[0], YH), bf16),
            pltpu.VMEM((2, LANES[0], YH), bf16),
            pltpu.VMEM((2, 2, 6, GROUP[0], YH), bf16),
            pltpu.VMEM((2, 2, 6, GROUP[0], YH), bf16),
            pltpu.VMEM((NX, SEG, TILE), f32),
            pltpu.VMEM((NX, SEG, TILE), f32),
            dma((2,)), dma((3,)), dma((3,)), dma((7,)), dma((7,)),
            dma((2, 2, 4)), dma((2, 2, 4)), dma((4,)), dma((4,)),
            dma((2,)), dma((2,)), dma((2, 2, 6)), dma((2, 2, 6)),
            dma((3,)), dma((3,)),
        ],
        compiler_params=pltpu.CompilerParams(
            collective_id=0, has_side_effects=True, vmem_limit_bytes=48 * 2**20),
    )(hx, hy)


def per_device(aux_tiles, orbitals, tile_rows, tile_cols, tile_count):
    hx, hy = half(aux_tiles, orbitals, tile_rows, tile_cols, tile_count)
    return exchange(hx, hy)


def solution(mesh):
    return jax.shard_map(
        per_device,
        mesh=mesh,
        in_specs=(
            P("aux", None, None, None),
            P("occ", None),
            P("aux", None),
            P("aux", None),
            P("aux"),
        ),
        out_specs=P("aux", "occ"),
        check_vma=False,
    )
```

time: 240 us -> 80.1 us (0.33)
  waiting for transfers between devices: 159 us -> 0 us
  Pallas kernels: 0 us -> 75.6 us
  local copies, waits for them, and re-layouts: 27.2 us -> 2.52 us
  blocking collectives: 23.4 us -> 0 us
  matrix products: 15.1 us -> 0 us
  between operations: 14.1 us -> 0.68 us
    all_gather x1 -> x0, waiting for transfers between devices: 95.7 us -> none  [per_device(): lax.all_gather(relaid, 'aux', axis=2, tiled=True)]
    pallas_call x0 -> x2, Pallas kernels: none -> 75.6 us  [the longest x1 68.5 us: exchange(): pl.pallas_call(exchange_kernel, out_shape=jax.ShapeDtypeStruct((ROWS, COL...]
    unnamed x3 -> x0, waiting for transfers between devices: 63.2 us -> none
    all_to_all x1 -> x0, blocking collectives: 23.4 us -> none  [per_device(): lax.all_to_all(half_vals, 'aux', split_axis=2, concat_axis=1, tiled=True)]
    dot_general x3 -> x0, matrix products: 15.1 us -> none  [the longest x1 8.78 us: per_device(): jnp.einsum('ipm,ipn->mn', relaid, lax.all_gather(relaid, 'aux', axis=2, t...]
    unnamed x7 -> x5, local copies, waits for them, and re-layouts: 14.2 us -> 2.52 us
    all_to_all x2 -> x0, local copies, waits for them, and re-layouts: 7.53 us -> none  [per_device(): lax.all_to_all(half_vals, 'aux', split_axis=2, concat_axis=1, tiled=True)]
    convert_element_type x1 -> x0, local copies, waits for them, and re-layouts: 4.78 us -> none  [per_device(): placed.reshape(occ_local, aux_tiles.shape[0], basis).astype(jnp.bfloat16)]
  transfers between devices with their start and end apart: 2 -> 0, of which waited for: 2 -> 0; matrix products, arithmetic and copies ran while one was open for 0% -> 0% of each run, Pallas kernels for 0% -> 0%
where the time goes in v2:
time: 80.1 us; the launch traced here: 78.8 us
  Pallas kernels  75.6 us (94%)
  local copies, waits for them, and re-layouts  2.52 us (3%)
    pallas_call x1, Pallas kernels, exchange(): pl.pallas_call(exchange_kernel, out_shape=jax.ShapeDtypeStruct((ROWS, COL...  68.5 us
    pallas_call x1, Pallas kernels, half(): pl.pallas_call(half_kernel, in_specs=[anywhere] * 5, out_specs=[vmem] * 2...  7.16 us
    unnamed x5, local copies, waits for them, and re-layouts  2.52 us

profile of v2, /device:TPU:6, one launch (start us, length us, event | category | flops | bytes accessed | tf_op | source)
XLA Modules:
  0.0 78.8 jit_solution(8076738051956209381)
XLA Ops:
  0.7 7.2 %shard_map.55 = (bf16[4,16,1408]{2,1,0:T(8,128)(2,1)}, bf16[8,16,768]{2,1,0:T(8,128)(2,1)}) custom-call(s32[1,64]{1,0:T(1,128)} %rows_hbm.1, s32[1,64]{1,0:T(1,128)} %cols_hbm.1, s32[1]{0:T(128)S(6)} %copy.7.count_hbm, bf16[4,64,128,128]{3,2,1,0:T(8,128)(2,1)} %tiles_hbm.1, bf16[4,5376]{1,0:T(4,128)(2,1)} %orb_hbm.1), custom_call_target="tpu_custom_call" | custom-call | tf_op jit(solution)/shard_map/pallas_call | solution.py:101
  7.8 0.0 copy-start
  7.8 0.9 %copy-done = bf16[8,16,768]{2,1,0:T(8,128)(2,1)S(1)} copy-done((bf16[8,16,768]{2,1,0:T(8,128)(2,1)S(1)}, bf16[8,16,768]{2,1,0:T(8,128)(2,1)}, u32[]{:S(2)}) %copy-start) | copy-done | bytes 196632
  8.7 0.0 copy-start.1
  8.8 0.9 %copy-done.1 = bf16[4,16,1408]{2,1,0:T(8,128)(2,1)S(1)} copy-done((bf16[4,16,1408]{2,1,0:T(8,128)(2,1)S(1)}, bf16[4,16,1408]{2,1,0:T(8,128)(2,1)}, u32[]{:S(2)}) %copy-start.1) | copy-done | bytes 180248
  9.7 68.5 %shard_map.56 = f32[84,448]{1,0:T(8,128)S(1)} custom-call(bf16[4,16,1408]{2,1,0:T(8,128)(2,1)S(1)} %copy-done.1, bf16[8,16,768]{2,1,0:T(8,128)(2,1)S(1)} %copy-done), custom_call_target="tpu_custom_call" | custom-call | tf_op jit(solution)/shard_map/pallas_call | solution.py:297
  78.1 0.7 copy.8
Async XLA Ops:
  7.8 0.9 %copy-start = (bf16[8,16,768]{2,1,0:T(8,128)(2,1)S(1)}, bf16[8,16,768]{2,1,0:T(8,128)(2,1)}, u32[]{:S(2)}) copy-start(bf16[8,16,768]{2,1,0:T(8,128)(2,1)} %get-tuple-element.8.hy_ref) | copy-start | bytes 589828
  8.7 0.9 %copy-start.1 = (bf16[4,16,1408]{2,1,0:T(8,128)(2,1)S(1)}, bf16[4,16,1408]{2,1,0:T(8,128)(2,1)}, u32[]{:S(2)}) copy-start(bf16[4,16,1408]{2,1,0:T(8,128)(2,1)} %get-tuple-element.7.hx_ref) | copy-start | bytes 540676

commit v3 on v2

v3 whole, which is shorter than its diff:
```python
import functools

import jax
import jax.numpy as jnp
from jax import lax
from jax.experimental import pallas as pl
from jax.experimental.pallas import tpu as pltpu
from jax.sharding import PartitionSpec as P

MESH = pl.DeviceIdType.MESH
TILE = 128
NB = 42
NT = 64
PD = 4
OL = 4
BASIS = NB * TILE
NX, NY, NC, NZ = 4, 8, 2, 12
ROWS = 84
COLS = 448
SEG = COLS // NX
GROUP = (32, 48, 32)
LANES = tuple(-(-NZ * size // TILE) * TILE for size in GROUP)
BASE = tuple(sum(LANES[:g]) for g in range(len(GROUP)))
START = tuple(sum(GROUP[:g]) for g in range(len(GROUP)))
NG = len(GROUP)
XW = sum(LANES)
YH = 384
YW = 2 * YH
KP = PD * OL
NBP = 48
CUT = 8
AHEAD = 3
QUICK = (((0, 1, False), (0, 2, False)), ((2, 1, False), (2, 2, True)))
LIGHT = (((0, 1, False),), ((1, 1, False),), ((2, 1, False), (2, 2, True)))
GATHER = (LIGHT, LIGHT, LIGHT)
THREE = ((5, 4), (3, 2), (4, 2), (2, 0), (1, 0))
TWO = ((4, 3), (5, 3), (3, 0), (2, 0), (1, 0))
EDGES = ((THREE + ((6, 4),), THREE),) * NG


def level(edges, node):
    return max((1 + level(edges, source) for source, target in edges if target == node), default=0)


def fetch(tiles_hbm, tiles, tile_sem, k):
    cut = pl.ds(k * CUT, CUT)
    return pltpu.make_async_copy(tiles_hbm.at[:, cut], tiles.at[:, cut], tile_sem.at[k])


def half(rows_v, cols_v, count_s, tiles_hbm, tiles, orb, by_block, chosen, tile_sem, copies, slots, placed, flat,
         hx_own, hy_own):
    for copy in copies:
        copy.wait()
    block_id = lax.broadcasted_iota(jnp.int32, (NBP, NT), 0)
    slot_id = lax.broadcasted_iota(jnp.int32, (NBP, NT), 1)
    by_block[...] = jnp.zeros_like(by_block)
    for b in range(NB):
        by_block[:, b, :] = orb[:, b * TILE:(b + 1) * TILE].astype(jnp.float32)
    hot = jnp.where(cols_v[...] == block_id, 1.0, 0.0).astype(jnp.bfloat16)
    for i in range(OL):
        chosen[i] = lax.dot_general(hot, by_block[i].astype(jnp.bfloat16), (((0,), (0,)), ((), ())),
                                    preferred_element_type=jnp.float32)
    for k in range(NT // CUT):
        fetch(tiles_hbm, tiles, tile_sem, k).wait()
        if k + AHEAD < NT // CUT:
            fetch(tiles_hbm, tiles, tile_sem, k + AHEAD).start()
        for t in range(k * CUT, (k + 1) * CUT):
            block = chosen[:, t, :].astype(jnp.bfloat16)
            tile = tiles[:, t].reshape(PD * TILE, TILE)
            got = lax.dot_general(block, tile, (((1,), (1,)), ((), ())), preferred_element_type=jnp.float32)
            for p in range(PD):
                slots[p * OL:(p + 1) * OL, t, :] = got[:, p * TILE:(p + 1) * TILE]
    hot = jnp.where((rows_v[...] == block_id) & (slot_id < count_s[0]), 1.0, 0.0).astype(jnp.bfloat16)
    hot = jnp.concatenate([hot, hot, hot], axis=1)
    for k in range(0, KP, 2):
        parts = []
        for j in (k, k + 1):
            value = slots[j]
            high = value.astype(jnp.bfloat16)
            rest = value - high.astype(jnp.float32)
            middle = rest.astype(jnp.bfloat16)
            low = (rest - middle.astype(jnp.float32)).astype(jnp.bfloat16)
            parts.append(jnp.concatenate([high, middle, low], axis=0))
        sums = jnp.dot(hot, jnp.concatenate(parts, axis=1), preferred_element_type=jnp.float32)
        placed[k] = sums[:, 0:TILE]
        placed[k + 1] = sums[:, TILE:2 * TILE]
    for b in range(NB):
        flat[:, b * TILE:(b + 1) * TILE] = placed[:, b, :]
    for x in range(NX):
        parts = []
        for g in range(NG):
            for o in range(NZ):
                a = o * COLS + x * SEG + START[g]
                parts.append(flat[:, a:a + GROUP[g]])
            if LANES[g] > NZ * GROUP[g]:
                parts.append(jnp.zeros((KP, LANES[g] - NZ * GROUP[g]), jnp.float32))
        hx_own[x] = jnp.concatenate(parts, axis=1).astype(jnp.bfloat16)
    for y in range(NY):
        parts = []
        for c in range(NC):
            for x in range(NX):
                a = ((y * NX + x) * NC + c) * ROWS
                parts.append(flat[:, a:a + ROWS])
            parts.append(jnp.zeros((KP, YH - NX * ROWS), jnp.float32))
        hy_own[y] = jnp.concatenate(parts, axis=1).astype(jnp.bfloat16)


def exchange_kernel(
    rows_hbm, cols_hbm, count_hbm, tiles_hbm, orb_hbm, out_ref,
    rows_v, cols_v, count_s, tiles, orb, by_block, chosen, slots, placed, flat, hx_ref, hy_ref,
    hx, hy, own, sib_out, sib_in, tree_out, tree_in, final_out, final_in,
    local_sem, tile_sem, x_send, x_recv, y_send, y_recv, ring_send, ring_recv, row_send, row_recv,
    sib_send, sib_recv, tree_send, tree_recv, fin_send, fin_recv,
):
    aux = lax.axis_index("aux")
    z = lax.axis_index("occ")
    c = lax.rem(aux, NC)
    x = lax.rem(aux // NC, NX)
    y = aux // (NC * NX)
    sign = 1 - 2 * c

    def at(y_, x_, c_, z_):
        return ((y_ * NX + x_) * NC + c_, z_)

    def xp(d):
        return lax.rem(x + d + NX, NX)

    def yp(d):
        return lax.rem(y + d + NY, NY)

    def zp(d):
        return lax.rem(z + sign * d + NZ, NZ)

    small = [
        pltpu.make_async_copy(rows_hbm, rows_v, local_sem.at[0]),
        pltpu.make_async_copy(cols_hbm, cols_v, local_sem.at[1]),
        pltpu.make_async_copy(count_hbm, count_s, local_sem.at[2]),
        pltpu.make_async_copy(orb_hbm, orb, local_sem.at[3]),
    ]
    for copy in small:
        copy.start()
    for k in range(AHEAD):
        fetch(tiles_hbm, tiles, tile_sem, k).start()
    partners = [at(y, xp(d), c, z) for d in range(1, NX)]
    partners += [at(yp(d), x, c, z) for d in range(1, NY)]
    partners += [at(y, x, c, zp(d)) for d in (1, 2, 3, -1, -2, -3)]
    partners += [at(y, x, 1 - c, z)]
    barrier = pltpu.get_barrier_semaphore()
    for partner in partners:
        pl.semaphore_signal(barrier, inc=1, device_id=partner, device_id_type=MESH)
    half(rows_v, cols_v, count_s, tiles_hbm, tiles, orb, by_block, chosen, tile_sem, small, slots, placed, flat, hx_ref, hy_ref)
    pl.semaphore_wait(barrier, len(partners))

    started = []

    def send(src, dst, s_sem, r_sem, device):
        copy = pltpu.make_async_remote_copy(
            src_ref=src, dst_ref=dst, send_sem=s_sem, recv_sem=r_sem, device_id=device, device_id_type=MESH)
        copy.start()
        started.append(copy)
        return copy

    def arrive(copies):
        for copy in copies:
            copy.wait_recv()

    to_x = [send(hx_ref.at[xp(d)], hx.at[y, x], x_send.at[d - 1], x_recv.at[d - 1], at(y, xp(d), c, z))
            for d in range(1, NX)]
    order = (1, 7, 2, 6, 3, 5, 4)
    to_y = {d: send(hy_ref.at[yp(d)], hy.at[y, x], y_send.at[d - 1], y_recv.at[d - 1], at(yp(d), x, c, z))
            for d in order}
    hx[y, x] = hx_ref[x]
    hy[y, x] = hy_ref[y]

    right, left = at(y, xp(1), c, z), at(y, xp(-1), c, z)
    row0, row1 = {}, {}

    def spread(d):
        piece_ref = hy.at[yp(-d), x]
        row0[d] = (send(piece_ref, piece_ref, row_send.at[0, d], row_recv.at[0, d], right),
                   send(piece_ref, piece_ref, row_send.at[1, d], row_recv.at[1, d], left))

    def pass_on(d):
        arrive(row0[d])
        way = d % 2
        piece_ref = hy.at[yp(-d), xp(1 if way else -1)]
        row1[d] = send(piece_ref, piece_ref, row_send.at[2, d], row_recv.at[2, d], left if way else right)

    spread(0)
    arrive(to_x)

    rings = {}

    def ring(g, stage):
        lanes = pl.ds(BASE[g], LANES[g])
        count = sum(len(s) for s in GATHER[g][:stage])
        copies = []
        for n, (behind, hops, halved) in enumerate(GATHER[g][stage]):
            for way, turn in ((0, 1), (1, -1)):
                chunk = yp(-turn * behind)
                if halved:
                    ref = hx.at[chunk, 2 * way:2 * way + 2, :, lanes]
                else:
                    ref = hx.at[chunk, :, :, lanes]
                copies.append(send(ref, ref, ring_send.at[way, g, count + n], ring_recv.at[way, g, count + n],
                                   at(yp(turn * hops), x, c, z)))
        rings[g, stage] = copies

    for g in range(NG):
        ring(g, 0)
    for d in order:
        arrive([to_y[d]])
        spread(d)
    arrive(rings[0, 0])
    ring(0, 1)
    for d in (0,) + order[:3]:
        pass_on(d)
    for g in range(1, NG):
        arrive(rings[g, 0])
        ring(g, 1)
    for d in order[3:]:
        pass_on(d)
    for g in range(NG):
        if len(GATHER[g]) > 2:
            arrive(rings[g, 1])
            ring(g, 2)
    arrive(row1.values())

    sibling = at(y, x, 1 - c, z)
    sib = {}

    def product(g, core, j):
        hx_all = hx[:, :, :, BASE[g] + j:BASE[g] + j + TILE].reshape(NY * NX * KP, TILE)
        hy_all = hy[:, :, :, pl.ds(pl.multiple_of(core * YH, TILE), YH)].reshape(NY * NX * KP, YH)
        return lax.dot_general(hx_all, hy_all, (((0,), (0,)), ((), ())), preferred_element_type=jnp.float32)

    def multiply(g):
        used = NZ * GROUP[g]
        for j in range(0, LANES[g], TILE):
            sib_out[g, j:j + TILE, :] = product(g, 1 - c, j).astype(jnp.bfloat16)
        sib[g] = send(sib_out.at[g, 0:used], sib_in.at[g, 0:used], sib_send.at[g], sib_recv.at[g], sibling)
        for j in range(0, LANES[g], TILE):
            own[g, j:j + TILE, :] = product(g, c, j)

    def add_sibling(g):
        used = NZ * GROUP[g]
        sib[g].wait_recv()
        own[g, 0:used, :] += sib_in[g, 0:used, :].astype(jnp.float32)

    trees = {}

    def piece(g, o):
        return own[g, pl.ds(pl.multiple_of(o * GROUP[g], 16), GROUP[g]), :]

    def gathered(g, way, node, value):
        for n, (source, target) in enumerate(EDGES[g][way]):
            if target == node:
                trees[g, way, n].wait_recv()
                value = value + tree_in[g, way, n, 0:GROUP[g], :].astype(jnp.float32)
        return value

    def tree(g, depth):
        for way, turn in ((0, 1), (1, -1)):
            edges = EDGES[g][way]
            for n, (source, target) in enumerate(edges):
                if level(edges, source) == depth:
                    value = gathered(g, way, source, piece(g, zp(-turn * source)))
                    tree_out[g, way, n, 0:GROUP[g], :] = value.astype(jnp.bfloat16)
                    trees[g, way, n] = send(
                        tree_out.at[g, way, n, 0:GROUP[g]], tree_in.at[g, way, n, 0:GROUP[g]],
                        tree_send.at[g, way, n], tree_recv.at[g, way, n], at(y, x, c, zp(-turn * (source - target))))

    for g in range(NG):
        arrive(rings[g, len(GATHER[g]) - 1])
        multiply(g)
        add_sibling(g)
        tree(g, 0)
    for depth in (1, 2):
        for g in range(NG):
            tree(g, depth)
    last = []
    for g in range(NG):
        value = piece(g, z)
        for way in range(2):
            value = gathered(g, way, 0, value)
        rows = pl.ds(START[g], GROUP[g])
        for q in range(NX):
            final_out[q, rows, 0:ROWS] = value[:, q * ROWS:(q + 1) * ROWS]
            final_out[q, rows, ROWS:TILE] = jnp.zeros((GROUP[g], TILE - ROWS), jnp.float32)
        last += [send(final_out.at[xp(d), rows], final_in.at[x, rows], fin_send.at[g, d - 1], fin_recv.at[g, d - 1],
                      at(y, xp(d), c, z)) for d in range(1, NX)]
        final_in[x, rows] = final_out[x, rows]
    arrive(last)
    out_ref[...] = final_in[...].reshape(COLS, TILE).T[0:ROWS]
    for copy in started:
        copy.wait_send()


def per_device(aux_tiles, orbitals, tile_rows, tile_cols, tile_count):
    anywhere = pl.BlockSpec(memory_space=pl.ANY)
    dma = pltpu.SemaphoreType.DMA
    f32, bf16 = jnp.float32, jnp.bfloat16
    most = max(LANES)
    return pl.pallas_call(
        exchange_kernel,
        out_shape=jax.ShapeDtypeStruct((ROWS, COLS), f32),
        in_specs=[anywhere] * 5,
        out_specs=pl.BlockSpec(memory_space=pltpu.VMEM),
        scratch_shapes=[
            pltpu.VMEM((1, NT), jnp.int32),
            pltpu.VMEM((1, NT), jnp.int32),
            pltpu.SMEM((1,), jnp.int32),
            pltpu.VMEM((PD, NT, TILE, TILE), bf16),
            pltpu.VMEM((OL, BASIS), bf16),
            pltpu.VMEM((OL, NBP, TILE), f32),
            pltpu.VMEM((OL, NT, TILE), f32),
            pltpu.VMEM((KP, NT, TILE), f32),
            pltpu.VMEM((KP, NBP, TILE), f32),
            pltpu.VMEM((KP, BASIS), f32),
            pltpu.VMEM((NX, KP, XW), bf16),
            pltpu.VMEM((NY, KP, YW), bf16),
            pltpu.VMEM((NY, NX, KP, XW), bf16),
            pltpu.VMEM((NY, NX, KP, YW), bf16),
            pltpu.VMEM((NG, most, YH), f32),
            pltpu.VMEM((NG, most, YH), bf16),
            pltpu.VMEM((NG, most, YH), bf16),
            pltpu.VMEM((NG, 2, 6, max(GROUP), YH), bf16),
            pltpu.VMEM((NG, 2, 6, max(GROUP), YH), bf16),
            pltpu.VMEM((NX, SEG, TILE), f32),
            pltpu.VMEM((NX, SEG, TILE), f32),
            dma((4,)), dma((NT // CUT,)), dma((3,)), dma((3,)), dma((7,)), dma((7,)),
            dma((2, NG, 4)), dma((2, NG, 4)), dma((3, NY)), dma((3, NY)),
            dma((NG,)), dma((NG,)), dma((NG, 2, 6)), dma((NG, 2, 6)),
            dma((NG, 3)), dma((NG, 3)),
        ],
        compiler_params=pltpu.CompilerParams(
            collective_id=0, has_side_effects=True, vmem_limit_bytes=56 * 2**20),
    )(tile_rows, tile_cols, tile_count, aux_tiles, orbitals)


def solution(mesh):
    return jax.shard_map(
        per_device,
        mesh=mesh,
        in_specs=(
            P("aux", None, None, None),
            P("occ", None),
            P("aux", None),
            P("aux", None),
            P("aux"),
        ),
        out_specs=P("aux", "occ"),
        check_vma=False,
    )
```

time: 80.1 us -> 68.1 us (0.85)
  Pallas kernels: 75.6 us -> 64.6 us
  local copies, waits for them, and re-layouts: 2.52 us -> 1.61 us
    pallas_call x2 -> x1, Pallas kernels: 75.6 us -> 64.6 us  [per_device(): pl.pallas_call(exchange_kernel, out_shape=jax.ShapeDtypeStruct((ROWS, COL...]
    unnamed x5 -> x1, local copies, waits for them, and re-layouts: 2.52 us -> 1.61 us
where the time goes in v3:
time: 68.1 us; the launch traced here: 66.9 us
  Pallas kernels  64.6 us (95%)
  local copies, waits for them, and re-layouts  1.61 us (2%)
    pallas_call x1, Pallas kernels, per_device(): pl.pallas_call(exchange_kernel, out_shape=jax.ShapeDtypeStruct((ROWS, COL...  64.6 us
    unnamed x1, local copies, waits for them, and re-layouts  1.61 us

profile of v3, /device:TPU:6, one launch (start us, length us, event | category | flops | bytes accessed | tf_op | source)
XLA Modules:
  0.0 66.9 jit_solution(11188127093058594141)
XLA Ops:
  0.7 64.6 %shard_map.55 = f32[84,448]{1,0:T(8,128)} custom-call(s32[1,64]{1,0:T(1,128)} %rows_hbm.1, s32[1,64]{1,0:T(1,128)} %cols_hbm.1, s32[1]{0:T(128)S(6)} %copy.7.count_hbm, bf16[4,64,128,128]{3,2,1,0:T(8,128)(2,1)} %tiles_hbm.1, bf16[4,5376]{1,0:T(4,128)(2,1)} %orb_hbm.1), custom_call_target="tpu_custom_call" | custom-call | tf_op jit(solution)/shard_map/pallas_call | solution.py:304
  65.3 1.6 %copy.8 = f32[84,448]{1,0:T(8,128)} copy(f32[84,448]{1,0:T(8,128)} %shard_map.55) | data formatting | bytes 301056

commit v4 on v3

--- a/solution.py
+++ b/solution.py
@@ -18,7 +18,7 @@
 ROWS = 84
 COLS = 448
 SEG = COLS // NX
-GROUP = (32, 48, 32)
+GROUP = (32, 32, 32, 16)
 LANES = tuple(-(-NZ * size // TILE) * TILE for size in GROUP)
 BASE = tuple(sum(LANES[:g]) for g in range(len(GROUP)))
 START = tuple(sum(GROUP[:g]) for g in range(len(GROUP)))
@@ -32,10 +32,10 @@
 AHEAD = 3
 QUICK = (((0, 1, False), (0, 2, False)), ((2, 1, False), (2, 2, True)))
 LIGHT = (((0, 1, False),), ((1, 1, False),), ((2, 1, False), (2, 2, True)))
-GATHER = (LIGHT, LIGHT, LIGHT)
-THREE = ((5, 4), (3, 2), (4, 2), (2, 0), (1, 0))
+GATHER = (LIGHT,) * NG
+THREE = ((5, 4), (3, 2), (1, 0), (4, 2), (2, 0))
 TWO = ((4, 3), (5, 3), (3, 0), (2, 0), (1, 0))
-EDGES = ((THREE + ((6, 4),), THREE),) * NG
+EDGES = ((((6, 4),) + THREE, THREE),) * NG
 
 
 def level(edges, node):
@@ -164,8 +164,11 @@
         for copy in copies:
             copy.wait_recv()
 
-    to_x = [send(hx_ref.at[xp(d)], hx.at[y, x], x_send.at[d - 1], x_recv.at[d - 1], at(y, xp(d), c, z))
-            for d in range(1, NX)]
+    def hand_out(part, lanes):
+        return [send(hx_ref.at[xp(d), :, lanes], hx.at[y, x, :, lanes], x_send.at[part, d - 1], x_recv.at[part, d - 1],
+                     at(y, xp(d), c, z)) for d in (1, 3, 2)]
+
+    to_x = [hand_out(0, pl.ds(0, LANES[0])), hand_out(1, pl.ds(LANES[0], XW - LANES[0]))]
     order = (1, 7, 2, 6, 3, 5, 4)
     to_y = {d: send(hy_ref.at[yp(d)], hy.at[y, x], y_send.at[d - 1], y_recv.at[d - 1], at(yp(d), x, c, z))
             for d in order}
@@ -187,7 +190,6 @@
         row1[d] = send(piece_ref, piece_ref, row_send.at[2, d], row_recv.at[2, d], left if way else right)
 
     spread(0)
-    arrive(to_x)
 
     rings = {}
 
@@ -206,7 +208,10 @@
                                    at(yp(turn * hops), x, c, z)))
         rings[g, stage] = copies
 
-    for g in range(NG):
+    arrive(to_x[0])
+    ring(0, 0)
+    arrive(to_x[1])
+    for g in range(1, NG):
         ring(g, 0)
     for d in order:
         arrive([to_y[d]])
@@ -260,10 +265,11 @@
         return value
 
     def tree(g, depth):
-        for way, turn in ((0, 1), (1, -1)):
-            edges = EDGES[g][way]
-            for n, (source, target) in enumerate(edges):
-                if level(edges, source) == depth:
+        for n in range(6):
+            for way, turn in ((0, 1), (1, -1)):
+                edges = EDGES[g][way]
+                if n < len(edges) and level(edges, edges[n][0]) == depth:
+                    source, target = edges[n]
                     value = gathered(g, way, source, piece(g, zp(-turn * source)))
                     tree_out[g, way, n, 0:GROUP[g], :] = value.astype(jnp.bfloat16)
                     trees[g, way, n] = send(
@@ -273,6 +279,11 @@
     for g in range(NG):
         arrive(rings[g, len(GATHER[g]) - 1])
         multiply(g)
+        if g == NG - 2:
+            continue
+        if g == NG - 1:
+            add_sibling(g - 1)
+            tree(g - 1, 0)
         add_sibling(g)
         tree(g, 0)
     for depth in (1, 2):
@@ -328,7 +339,7 @@
             pltpu.VMEM((NG, 2, 6, max(GROUP), YH), bf16),
             pltpu.VMEM((NX, SEG, TILE), f32),
             pltpu.VMEM((NX, SEG, TILE), f32),
-            dma((4,)), dma((NT // CUT,)), dma((3,)), dma((3,)), dma((7,)), dma((7,)),
+            dma((4,)), dma((NT // CUT,)), dma((2, 3)), dma((2, 3)), dma((7,)), dma((7,)),
             dma((2, NG, 4)), dma((2, NG, 4)), dma((3, NY)), dma((3, NY)),
             dma((NG,)), dma((NG,)), dma((NG, 2, 6)), dma((NG, 2, 6)),
             dma((NG, 3)), dma((NG, 3)),

time: 68.1 us -> 67.2 us (0.987)
  the two profiles are of different devices: /device:TPU:6 before, /device:TPU:73 now
where the time goes in v4:
time: 67.2 us; the launch traced here: 67 us
  Pallas kernels  64.8 us (96%)
  local copies, waits for them, and re-layouts  1.61 us (2%)
    pallas_call x1, Pallas kernels, per_device(): pl.pallas_call(exchange_kernel, out_shape=jax.ShapeDtypeStruct((ROWS, COL...  64.8 us
    unnamed x1, local copies, waits for them, and re-layouts  1.61 us

profile of v4, /device:TPU:73, one launch (start us, length us, event | category | flops | bytes accessed | tf_op | source)
XLA Modules:
  0.0 67.0 jit_solution(6980333139668204075)
XLA Ops:
  0.7 64.8 %shard_map.55 = f32[84,448]{1,0:T(8,128)} custom-call(s32[1,64]{1,0:T(1,128)} %rows_hbm.1, s32[1,64]{1,0:T(1,128)} %cols_hbm.1, s32[1]{0:T(128)S(6)} %copy.7.count_hbm, bf16[4,64,128,128]{3,2,1,0:T(8,128)(2,1)} %tiles_hbm.1, bf16[4,5376]{1,0:T(4,128)(2,1)} %orb_hbm.1), custom_call_target="tpu_custom_call" | custom-call | tf_op jit(solution)/shard_map/pallas_call | solution.py:315
  65.4 1.6 %copy.8 = f32[84,448]{1,0:T(8,128)} copy(f32[84,448]{1,0:T(8,128)} %shard_map.55) | data formatting | bytes 301056

commit v5 on v4

--- a/solution.py
+++ b/solution.py
@@ -28,8 +28,8 @@
 YW = 2 * YH
 KP = PD * OL
 NBP = 48
-CUT = 8
-AHEAD = 3
+CUT = 16
+AHEAD = 2
 QUICK = (((0, 1, False), (0, 2, False)), ((2, 1, False), (2, 2, True)))
 LIGHT = (((0, 1, False),), ((1, 1, False),), ((2, 1, False), (2, 2, True)))
 GATHER = (LIGHT,) * NG
@@ -143,7 +143,7 @@
         fetch(tiles_hbm, tiles, tile_sem, k).start()
     partners = [at(y, xp(d), c, z) for d in range(1, NX)]
     partners += [at(yp(d), x, c, z) for d in range(1, NY)]
-    partners += [at(y, x, c, zp(d)) for d in (1, 2, 3, -1, -2, -3)]
+    partners += [at(y, x, c, zp(d)) for d in (1, 2, -1, -2)]
     partners += [at(y, x, 1 - c, z)]
     barrier = pltpu.get_barrier_semaphore()
     for partner in partners:

time: 67.2 us -> 66.6 us (level)
  Pallas kernels: 64.8 us -> 64.1 us
where the time goes in v5:
time: 66.6 us; the launch traced here: 66.4 us
  Pallas kernels  64.1 us (96%)
  local copies, waits for them, and re-layouts  1.61 us (2%)
    pallas_call x1, Pallas kernels, per_device(): pl.pallas_call(exchange_kernel, out_shape=jax.ShapeDtypeStruct((ROWS, COL...  64.1 us
    unnamed x1, local copies, waits for them, and re-layouts  1.61 us

profile of v5, /device:TPU:73, one launch (start us, length us, event | category | flops | bytes accessed | tf_op | source)
XLA Modules:
  0.0 66.4 jit_solution(16851261773187983910)
XLA Ops:
  0.7 64.1 %shard_map.55 = f32[84,448]{1,0:T(8,128)} custom-call(s32[1,64]{1,0:T(1,128)} %rows_hbm.1, s32[1,64]{1,0:T(1,128)} %cols_hbm.1, s32[1]{0:T(128)S(6)} %copy.7.count_hbm, bf16[4,64,128,128]{3,2,1,0:T(8,128)(2,1)} %tiles_hbm.1, bf16[4,5376]{1,0:T(4,128)(2,1)} %orb_hbm.1), custom_call_target="tpu_custom_call" | custom-call | tf_op jit(solution)/shard_map/pallas_call | solution.py:315
  64.8 1.6 %copy.8 = f32[84,448]{1,0:T(8,128)} copy(f32[84,448]{1,0:T(8,128)} %shard_map.55) | data formatting | bytes 301056
